TPU v7x, 512 devices: a whole 4x8x8 slice. The times are simulated.
512 devices in a mesh: row: 16 (over z_hi, y), col: 32 (over x, z_lo, core).
Axes of the slice: x: 4, y: 8, z: 8 (z_hi: 2, z_lo: 4; z = z_hi * 4 + z_lo), core: 2. Of those that a mesh axis runs over, the one named last changes fastest.
Arguments:
- cov_tiles: float32 [2, 16, 1, 32, 512, 512], P(None, 'row', None, 'col'), may hold values from -6 to 6
- inverse_factors: float32 [2, 512, 512], P(None, 'row'), may hold values from -0.3 to 0.3, as said below
- band: int32 [32], replicated, may hold values from 1 to 24, as said below
- station_noise: float32 [16384], replicated, may hold values from 0.5 to 4
- morton: int32 [16384], replicated, may hold values from 0 to 16383, each once
Outputs:
- factor_window: float32 [2, 16, 1, 32, 512, 512], P(None, 'row', None, 'col')
Inputs may be any that keep to these rules, and one draw needn't show every extreme that they name: `inverse_factors`: each matrix is upper triangular with a positive diagonal. Some row of tiles has a band of exactly 24.
All inputs are finite; a program needn't handle non-finite values.
Results may differ from a plain program's by a relative error of at most 0.0003.
Values sent between devices are 32-bit elements; how exact they have to be, the bound alone decides.
A program may use at most 64 MiB of HBM per device.

v0:
```python
import jax
import jax.numpy as jnp
from jax import lax
from jax.sharding import PartitionSpec as P

STEPS = 2


def spread(value, axis, source):
    kept = jnp.where(lax.axis_index(axis) == source, value, 0).astype(value.dtype)
    return lax.psum(kept, axis)


def on_device(cov_tiles, inverse_factors, band, station_noise, morton):
    grid_rows = lax.axis_size("row")
    grid_cols = lax.axis_size("col")
    own_row = lax.axis_index("row")
    own_col = lax.axis_index("col")
    blocks = cov_tiles[:, 0, :, 0]
    tile_rows = blocks.shape[0]
    tile_cols = blocks.shape[1]
    tile_size = blocks.shape[2]
    tile_count = band.shape[0]
    row_ids = jnp.arange(tile_rows, dtype=jnp.int32) * grid_rows + own_row
    col_ids = jnp.arange(tile_cols, dtype=jnp.int32) * grid_cols + own_col
    every_tile = jnp.arange(tile_count, dtype=jnp.int32)
    row_band = jnp.sum(jnp.where(every_tile[None, :] == row_ids[:, None], band[None, :], 0), axis=1)
    kept_mask = (col_ids[None, :] <= row_ids[:, None]) & (
        row_ids[:, None] - col_ids[None, :] <= row_band[:, None]
    )
    blocks = jnp.where(kept_mask[:, :, None, None], blocks, 0.0)
    is_diagonal = col_ids[None, :] == row_ids[:, None]
    mirrored = jnp.tril(blocks) + jnp.swapaxes(jnp.tril(blocks, -1), -1, -2)
    station_rows = morton.reshape(tile_count, tile_size)[row_ids]
    nugget = station_noise[station_rows]
    identity = jnp.eye(tile_size, dtype=jnp.float32)
    mirrored = mirrored + nugget[:, None, :, None] * identity
    blocks = jnp.where(is_diagonal[:, :, None, None], mirrored, blocks)
    for panel_step in range(STEPS):
        factor = lax.all_gather(inverse_factors[panel_step], "row", axis=0, tiled=True)
        owner_col = panel_step % grid_cols
        owner_slot = panel_step // grid_cols

        def make_factor(column):
            return jnp.einsum(
                "amn,np->amp",
                column,
                factor,
                precision=lax.Precision.HIGHEST,
                preferred_element_type=jnp.float32,
            )

        column = blocks[:, owner_slot]
        row_factor = lax.cond(own_col == owner_col, make_factor, jnp.zeros_like, column)
        row_factor = jnp.where((row_ids > panel_step)[:, None, None], row_factor, 0.0)
        row_factor = spread(row_factor, "col", owner_col)
        blocks = blocks.at[:, owner_slot].set(jnp.where(own_col == owner_col, row_factor, column))
        target = 0 + own_col
        held_tile = lax.dynamic_index_in_dim(row_factor, target // grid_rows, 0, keepdims=False)
        pieces = [spread(held_tile, "row", target % grid_rows)]
        col_factor = jnp.stack(pieces)
        update = jnp.einsum(
            "amp,bnp->abmn",
            row_factor,
            col_factor,
            precision=lax.Precision.HIGHEST,
            preferred_element_type=jnp.float32,
        )
        active = (col_ids[None, :] > panel_step) & (col_ids[None, :] <= row_ids[:, None])
        blocks = blocks - jnp.where(active[:, :, None, None], update, 0.0)
    return blocks[:, None, :, None]


def solution(mesh):
    placed = (P(None, "row", None, "col", None, None), P(None, "row", None), P(), P(), P())
    return jax.shard_map(
        on_device,
        mesh=mesh,
        in_specs=placed,
        out_specs=P(None, "row", None, "col", None, None),
        check_vma=False,
    )
```

profile of v0, /device:TPU:2, one launch (start us, length us, event | category | flops | bytes accessed | tf_op | source)
XLA Modules:
  0.0 1189.5 jit_solution(2500794160252668181)
XLA Ops:
  6.5 0.0 copy-start
  6.5 0.0 all-gather.5.cloned.1.call-start
  6.5 1.6 fusion.13
  8.1 0.0 all-gather.5.cloned.1.call-update
  8.1 0.0 all-reduce.5.cloned.1.call-start
  8.2 0.8 fusion.11
  9.1 1.9 bitcast_select_fusion.2
  11.0 0.0 copy-start.4
  11.0 1.8 copy.21
  12.8 0.0 copy-done.4
  12.8 0.6 gather_fusion
  13.4 0.0 copy-done
  13.4 0.0 copy-start.1
  13.4 6.2 gather_fusion.1
  19.6 0.2 iota_compare_fusion.2
  19.8 0.2 iota_compare_fusion.1
  20.1 0.0 copy-done.1
  20.1 3.7 fusion.6
  23.7 2.9 copy.23
  26.7 3.5 select_bitcast_fusion
  30.1 78.5 %all-gather.5.cloned.1.call-done = f32[1,512,512]{2,1,0:T(8,128)} async-done(((f32[1,32,512]{2,1,0:T(8,128)}), f32[1,512,512]{2,1,0:T(8,128)}) %all-gather.5.cloned.1.call-update) | async-done | bytes 1048592 | tf_op jit(solution)/shard_map/all_gather | solution.py:40
  108.6 0.3 conditional.2
  108.6 0.2 broadcast.314
  108.9 1.7 select_select_fusion.1
  110.6 0.0 all-reduce.5.cloned.1.call-update
  110.6 0.0 copy-start.2
  110.6 0.0 all-reduce.7.cloned.1.call-start
  110.7 269.9 %all-reduce.5.cloned.1.call-done = f32[2,512,512]{2,1,0:T(8,128)} async-done(((f32[2,512,512]{2,1,0:T(8,128)}), f32[2,512,512]{2,1,0:T(8,128)}) %all-reduce.5.cloned.1.call-update) | async-done | bytes 2097168 | tf_op jit(solution)/shard_map/psum | solution.py:11
  380.6 2.3 select_bitcast_fusion.2
  382.9 0.0 all-reduce.7.cloned.1.call-update
  382.9 0.0 all-gather.7.cloned.1.call-start
  383.0 0.5 all-gather.7.cloned.1.call-update
  383.5 0.0 all-reduce.9.cloned.1.call-start
  383.6 211.9 %all-reduce.7.cloned.1.call-done = f32[512,512]{1,0:T(8,128)} async-done(((f32[512,512]{1,0:T(8,128)}), f32[512,512]{1,0:T(8,128)}) %all-reduce.7.cloned.1.call-update) | async-done | bytes 1048592 | tf_op jit(solution)/shard_map/psum | solution.py:11
  595.5 7.4 fusion.5
  602.9 86.3 %all-gather.7.cloned.1.call-done = f32[1,512,512]{2,1,0:T(8,128)} async-done(((f32[1,32,512]{2,1,0:T(8,128)}), f32[1,512,512]{2,1,0:T(8,128)}) %all-gather.7.cloned.1.call-update) | async-done | bytes 1048592 | tf_op jit(solution)/shard_map/all_gather | solution.py:40
  689.2 0.4 conditional.3
  689.2 0.2 broadcast.315
  689.7 1.7 select_select_fusion
  691.4 0.0 all-reduce.9.cloned.1.call-update
  691.4 0.0 copy-start.3
  691.5 0.0 all-reduce.11.cloned.1.call-start
  691.5 268.7 %all-reduce.9.cloned.1.call-done = f32[2,512,512]{2,1,0:T(8,128)} async-done(((f32[2,512,512]{2,1,0:T(8,128)}), f32[2,512,512]{2,1,0:T(8,128)}) %all-reduce.9.cloned.1.call-update) | async-done | bytes 2097168 | tf_op jit(solution)/shard_map/psum | solution.py:11
  960.3 2.3 select_bitcast_fusion.1
  962.6 0.0 all-reduce.11.cloned.1.call-update
  962.6 212.6 %all-reduce.11.cloned.1.call-done = f32[512,512]{1,0:T(8,128)} async-done(((f32[512,512]{1,0:T(8,128)}), f32[512,512]{1,0:T(8,128)}) %all-reduce.11.cloned.1.call-update) | async-done | bytes 1048592 | tf_op jit(solution)/shard_map/psum | solution.py:11
  1175.2 0.0 copy-done.3
  1175.2 7.4 fusion.4
  (15 shorter events, 0.1 us)
Async XLA Ops:
  6.5 6.9 copy-start
  6.5 102.1 %all-gather.5.cloned.1.call-start = ((), (), s32[]{:S(2)}) async-start(), calls=%async_computation.4 | async-start | bytes 1114112 | tf_op jit(solution)/shard_map/all_gather | solution.py:40
  8.1 372.5 %all-reduce.5.cloned.1.call-start = ((), (), s32[]{:S(2)}) async-start(), calls=%async_computation | async-start | bytes 4194304 | tf_op jit(solution)/shard_map/psum | solution.py:11
  11.0 1.8 copy-start.4
  13.4 6.6 copy-start.1
  110.6 484.9 %copy-start.2 = (f32[2,512,512]{2,1,0:T(8,128)S(1)}, f32[2,512,512]{2,1,0:T(8,128)}, u32[]{:S(2)}) copy-start(f32[2,512,512]{2,1,0:T(8,128)} %select_bitcast_fusion) | copy-start | bytes 6291460
  110.6 484.9 %all-reduce.7.cloned.1.call-start = ((), (), s32[]{:S(2)}) async-start(), calls=%async_computation.1 | async-start | bytes 2097152 | tf_op jit(solution)/shard_map/psum | solution.py:11
  382.9 306.3 %all-gather.7.cloned.1.call-start = ((), (), s32[]{:S(2)}) async-start(), calls=%async_computation.5 | async-start | bytes 1114112 | tf_op jit(solution)/shard_map/all_gather | solution.py:40
  383.5 576.7 %all-reduce.9.cloned.1.call-start = ((), (), s32[]{:S(2)}) async-start(), calls=%async_computation.2 | async-start | bytes 4194304 | tf_op jit(solution)/shard_map/psum | solution.py:11
  691.4 483.8 %copy-start.3 = (f32[2,512,512]{2,1,0:T(8,128)S(1)}, f32[2,512,512]{2,1,0:T(8,128)}, u32[]{:S(2)}) copy-start(f32[2,512,512]{2,1,0:T(8,128)} %fusion.5) | copy-start | bytes 6291460
  691.5 483.8 %all-reduce.11.cloned.1.call-start = ((), (), s32[]{:S(2)}) async-start(), calls=%async_computation.3 | async-start | bytes 2097152 | tf_op jit(solution)/shard_map/psum | solution.py:11
Sparse Core Ops, SparseCore 0:
  10.6 97.9 all-gather.4
  111.5 269.0 all-reduce.4
  383.8 211.6 all-reduce.6
  598.6 90.6 all-gather.6
  692.0 268.2 all-reduce.8
  963.3 211.8 all-reduce.10
where the time goes:
time: 1190 us
  waiting for transfers between devices  1130 us (95%)
  other arithmetic  18.4 us (2%)
  matrix products  14.8 us (1%)
  between operations  13.7 us (1%)
  local copies, waits for them, and re-layouts  13.5 us (1%)
    psum x4, waiting for transfers between devices, spread(): return lax.psum(kept, axis)  963 us
    all_gather x2, waiting for transfers between devices, on_device(): lax.all_gather(inverse_factors[panel_step], 'row', axis=0, tiled=True)  165 us
  transfers between devices with their start and end apart: 6, of which 6 were waited for; matrix products, arithmetic and copies ran while one was open for 2% of the time, Pallas kernels for 0%

commit v1 on v0

--- a/solution.py
+++ b/solution.py
@@ -37,7 +37,12 @@
     mirrored = mirrored + nugget[:, None, :, None] * identity
     blocks = jnp.where(is_diagonal[:, :, None, None], mirrored, blocks)
     for panel_step in range(STEPS):
-        factor = lax.all_gather(inverse_factors[panel_step], "row", axis=0, tiled=True)
+        factor = jnp.concatenate(
+            lax.all_to_all(
+                jnp.stack([inverse_factors[panel_step]] * lax.axis_size("row")), "row", 0, 0
+            ),
+            axis=0,
+        )
         owner_col = panel_step % grid_cols
         owner_slot = panel_step // grid_cols
 

time: 1190 us -> 1070 us (0.90)
  waiting for transfers between devices: 1130 us -> 988 us
  starting transfers between devices: 0.21 us -> 23 us
    all_gather x2 -> x0, waiting for transfers between devices: 165 us -> none  [on_device(): lax.all_gather(inverse_factors[panel_step], 'row', axis=0, tiled=True)]
    all_to_all x0 -> x2, starting transfers between devices: none -> 22.9 us  [on_device(): lax.all_to_all(jnp.stack([inverse_factors[panel_step]] * lax.axis_size('r...]
    psum x4, waiting for transfers between devices: 963 us -> 979 us  [spread(): return lax.psum(kept, axis)]
  transfers between devices with their start and end apart: 6 -> 6, of which waited for: 6 -> 5; matrix products, arithmetic and copies ran while one was open for 2% -> 3% of each run, Pallas kernels for 0% -> 0%
where the time goes in v1:
time: 1070 us
  waiting for transfers between devices  988 us (92%)
  starting transfers between devices  23 us (2%)
  other arithmetic  17.5 us (2%)
  local copies, waits for them, and re-layouts  16.3 us (2%)
  matrix products  14.8 us (1%)
  between operations  13.4 us (1%)
    psum x4, waiting for transfers between devices, spread(): return lax.psum(kept, axis)  979 us
    all_to_all x2, starting transfers between devices, on_device(): lax.all_to_all(jnp.stack([inverse_factors[panel_step]] * lax.axis_size('r...  22.9 us
  transfers between devices with their start and end apart: 6, of which 5 were waited for; matrix products, arithmetic and copies ran while one was open for 3% of the time, Pallas kernels for 0%

profile of v1, /device:TPU:2, one launch (start us, length us, event | category | flops | bytes accessed | tf_op | source)
XLA Modules:
  0.0 1073.3 jit_solution(18370270077272132258)
XLA Ops:
  6.5 0.0 copy-start
  6.5 1.0 slice_bitcast_fusion
  7.6 1.1 stack.9
  8.7 15.6 %all-to-all-start.1 = ((f32[16,32,512]{2,1,0:T(8,128)}), f32[16,32,512]{2,1,0:T(8,128)S(1)}, u32[]{:S(2)}, u32[]{:S(2)}) async-start(f32[16,32,512]{2,1,0:T(8,128)} %stack.9), calls=%async_computation.1 | async-start | bytes 2097152 | tf_op jit(solution)/shard_map/all_to_all | solution.py:41
  24.3 0.0 all-reduce.5.cloned.1.call-start
  24.4 0.0 copy-done.5
  24.4 0.2 fusion.7
  24.6 0.0 copy-done.1
  24.6 1.6 bitcast_select_fusion.2
  26.3 2.9 copy.21
  29.2 0.0 copy-done.4
  29.2 0.6 gather_fusion
  29.8 0.0 copy-done
  29.8 6.2 gather_fusion.1
  36.0 0.2 iota_compare_fusion.2
  36.2 0.2 iota_compare_fusion.1
  36.4 3.7 fusion.2
  40.1 2.9 copy.23
  43.0 3.5 select_bitcast_fusion
  46.5 9.2 all-to-all-done.1
  55.7 0.3 conditional.2
  55.7 0.2 broadcast.316
  55.9 1.7 select_select_fusion.1
  57.7 0.0 all-reduce.5.cloned.1.call-update
  57.7 1.1 stack.8
  58.8 7.2 all-to-all-start
  66.0 0.0 copy-start.2
  66.0 0.0 all-reduce.7.cloned.1.call-start
  66.1 281.2 %all-reduce.5.cloned.1.call-done = f32[2,512,512]{2,1,0:T(8,128)} async-done(((f32[2,512,512]{2,1,0:T(8,128)}), f32[2,512,512]{2,1,0:T(8,128)}) %all-reduce.5.cloned.1.call-update) | async-done | bytes 2097168 | tf_op jit(solution)/shard_map/psum | solution.py:11
  347.3 2.3 select_bitcast_fusion.2
  349.7 0.0 all-reduce.7.cloned.1.call-update
  349.7 0.0 all-reduce.9.cloned.1.call-start
  349.8 212.8 %all-reduce.7.cloned.1.call-done = f32[512,512]{1,0:T(8,128)} async-done(((f32[512,512]{1,0:T(8,128)}), f32[512,512]{1,0:T(8,128)}) %all-reduce.7.cloned.1.call-update) | async-done | bytes 1048592 | tf_op jit(solution)/shard_map/psum | solution.py:11
  562.5 0.0 copy-done.2
  562.5 7.4 fusion.1
  569.9 0.0 all-to-all-done
  569.9 0.4 conditional.3
  569.9 0.2 broadcast.317
  570.4 1.7 select_select_fusion
  572.1 0.0 all-reduce.9.cloned.1.call-update
  572.1 0.0 copy-start.3
  572.1 0.0 all-reduce.11.cloned.1.call-start
  572.2 272.3 %all-reduce.9.cloned.1.call-done = f32[2,512,512]{2,1,0:T(8,128)} async-done(((f32[2,512,512]{2,1,0:T(8,128)}), f32[2,512,512]{2,1,0:T(8,128)}) %all-reduce.9.cloned.1.call-update) | async-done | bytes 2097168 | tf_op jit(solution)/shard_map/psum | solution.py:11
  844.4 2.3 select_bitcast_fusion.1
  846.8 0.0 all-reduce.11.cloned.1.call-update
  846.8 212.6 %all-reduce.11.cloned.1.call-done = f32[512,512]{1,0:T(8,128)} async-done(((f32[512,512]{1,0:T(8,128)}), f32[512,512]{1,0:T(8,128)}) %all-reduce.11.cloned.1.call-update) | async-done | bytes 1048592 | tf_op jit(solution)/shard_map/psum | solution.py:11
  1059.4 0.0 copy-done.3
  1059.4 7.4 fusion
  (16 shorter events, 0.1 us)
Async XLA Ops:
  6.5 23.3 %copy-start = (f32[16384]{0:T(1024)S(1)}, f32[16384]{0:T(1024)}, u32[]{:S(2)}) copy-start(f32[16384]{0:T(1024)} %param.16) | copy-start | bytes 196612
  6.5 17.9 %copy-start.5 = (s32[32]{0:T(128)S(1)}, s32[32]{0:T(128)}, u32[]{:S(2)}) copy-start(s32[32]{0:T(128)} %param.15) | copy-start | bytes 388
  6.5 18.1 %copy-start.1 = (f32[2,1,1,1,512,512]{5,4,3,2,1,0:T(8,128)S(1)}, f32[2,1,1,1,512,512]{5,4,3,2,1,0:T(8,128)}, u32[]{:S(2)}) copy-start(f32[2,1,1,1,512,512]{5,4,3,2,1,0:T(8,128)} %param.13) | copy-start | bytes 6291460
  8.7 47.0 %all-to-all-start.1 = ((f32[16,32,512]{2,1,0:T(8,128)}), f32[16,32,512]{2,1,0:T(8,128)S(1)}, u32[]{:S(2)}, u32[]{:S(2)}) async-start(f32[16,32,512]{2,1,0:T(8,128)} %stack.9), calls=%async_computation.1 | async-start | bytes 2097152 | tf_op jit(solution)/shard_map/all_to_all | solution.py:41
  24.3 323.0 %all-reduce.5.cloned.1.call-start = ((), (), s32[]{:S(2)}) async-start(), calls=%async_computation.2 | async-start | bytes 4194304 | tf_op jit(solution)/shard_map/psum | solution.py:11
  26.3 2.9 copy-start.4
  58.8 511.1 %all-to-all-start = ((f32[16,32,512]{2,1,0:T(8,128)}), f32[16,32,512]{2,1,0:T(8,128)S(1)}, u32[]{:S(2)}, u32[]{:S(2)}) async-start(f32[16,32,512]{2,1,0:T(8,128)} %stack.8), calls=%async_computation | async-start | bytes 2097152 | tf_op jit(solution)/shard_map/all_to_all | solution.py:41
  66.0 496.5 %copy-start.2 = (f32[2,512,512]{2,1,0:T(8,128)S(1)}, f32[2,512,512]{2,1,0:T(8,128)}, u32[]{:S(2)}) copy-start(f32[2,512,512]{2,1,0:T(8,128)} %select_bitcast_fusion) | copy-start | bytes 6291460
  66.0 496.5 %all-reduce.7.cloned.1.call-start = ((), (), s32[]{:S(2)}) async-start(), calls=%async_computation.3 | async-start | bytes 2097152 | tf_op jit(solution)/shard_map/psum | solution.py:11
  349.7 494.8 %all-reduce.9.cloned.1.call-start = ((), (), s32[]{:S(2)}) async-start(), calls=%async_computation.4 | async-start | bytes 4194304 | tf_op jit(solution)/shard_map/psum | solution.py:11
  572.1 487.3 %copy-start.3 = (f32[2,512,512]{2,1,0:T(8,128)S(1)}, f32[2,512,512]{2,1,0:T(8,128)}, u32[]{:S(2)}) copy-start(f32[2,512,512]{2,1,0:T(8,128)} %fusion.1) | copy-start | bytes 6291460
  572.1 487.3 %all-reduce.11.cloned.1.call-start = ((), (), s32[]{:S(2)}) async-start(), calls=%async_computation.5 | async-start | bytes 2097152 | tf_op jit(solution)/shard_map/psum | solution.py:11
Sparse Core Ops, SparseCore 0:
  57.8 289.4 all-reduce.4
  350.5 211.9 all-reduce.6
  572.2 272.1 all-reduce.8
  847.5 211.8 all-reduce.10
